TPU v7x, 512 devices: a whole 4x4x16 slice. The times are simulated.
512 devices in a mesh: red: 64 (over z, y), rep: 8 (over x, core).
Axes of the slice: x: 4, y: 4, z: 16, core: 2. Of those that a mesh axis runs over, the one named last changes fastest.
Arguments:
- amplitudes: bfloat16 [7680, 960, 120], P(('rep', 'red')), may hold values from -6 to 6
- integrals: bfloat16 [960, 120, 8, 120], P('red', None, 'rep'), may hold values from -0.046875 to 0.046875
- other_terms: float32 [7680, 8, 120], P(('rep', 'red')), may hold values from -6 to 6
- occ_energy: float32 [120], replicated, may hold values from -2 to -0.5
- vir_energy: float32 [960], replicated, may hold values from 0.5 to 3
- occ_irrep: int32 [120], replicated, may hold values from 0 to 7, as said below
- vir_irrep: int32 [960], replicated, may hold values from 0 to 7, as said below
- slab_a: int32 [1], replicated, may hold values from 0 to 14
- slab_b: int32 [1], replicated, may hold values from 0 to 119
Outputs:
- new_amplitudes: float32 [7680, 8, 120], P(('rep', 'red'))
Inputs may be any that keep to these rules, and one draw needn't show every extreme that they name: `occ_irrep`: labels are nondecreasing over the orbitals (orbitals ordered by irrep); the first is 0 and the last is 7. `vir_irrep`: labels are nondecreasing over the orbitals (orbitals ordered by irrep); the first is 0 and the last is 7.
All inputs are finite; a program needn't handle non-finite values.
Results may differ from a plain program's by a relative error of at most 0.0003.
Values may be sent and summed in bfloat16 or wider, within the bound.
No kernel may reach another device: no remote copies, remote signals or barrier semaphores. Data moves between devices by JAX's collectives and lax.ppermute only.
A program may use at most 64 MiB of HBM per device.

v0:
```python
import functools

import jax
import jax.numpy as jnp
from jax import lax
from jax.experimental import pallas as pl
from jax.experimental.pallas import tpu as pltpu
from jax.sharding import Mesh, PartitionSpec as P

A = 64
B = 8
O = 120
V = 960
ROWS = 15
SLOTS = 24
GROUP = 5
PARTS = ROWS // GROUP
STEP = 5
FAR = 8
NEAR = 8
ACROSS = 4
SHARE = SLOTS // ACROSS
TEAM = NEAR * ACROSS
BLOCK = 32
STACK = 4
TWICE = FAR // STACK
DEEP = TWICE * PARTS
REP = 8
LANES = 128
BF = jnp.bfloat16
F32 = jnp.float32


def pair_labels(left, right):
    return jnp.bitwise_xor(left[:, None], right[None, :])


def column_of(row):
    n = row.shape[1]
    same = lax.broadcasted_iota(jnp.int32, (n, n), 0) == lax.broadcasted_iota(jnp.int32, (n, n), 1)
    return jnp.sum(jnp.where(same, row.astype(F32), 0.0), axis=1, keepdims=True).astype(jnp.int32)


def positions(occ_row):
    n = occ_row.shape[1]
    occ_col = column_of(occ_row)
    k_col = lax.broadcasted_iota(jnp.int32, (n, n), 0)
    k_row = lax.broadcasted_iota(jnp.int32, (n, n), 1)
    same = occ_col == occ_row
    row = jnp.sum(jnp.where(same & (k_col < k_row), 1.0, 0.0), axis=0, keepdims=True)
    col = jnp.sum(jnp.where(same & (k_row < k_col), 1.0, 0.0), axis=1, keepdims=True)
    return occ_col, row.astype(jnp.int32), col.astype(jnp.int32)


def thirds(x):
    high = x.astype(BF)
    rest = x - high.astype(F32)
    middle = rest.astype(BF)
    low = (rest - middle.astype(F32)).astype(BF)
    return high, middle, low


def pack_integrals(place, window, vir_irrep, slab_b, occ_row, integrals, out, most, scratch):
    red, rep = place()
    occ = occ_row[...]
    occ_col, pos_row, _ = positions(occ)
    most[0, 0] = jnp.max(pos_row)
    slot = lax.broadcasted_iota(jnp.int32, (SLOTS, O), 0)
    pick = jnp.where(slot == pos_row - SLOTS * window, 1.0, 0.0).astype(BF)
    b_label = vir_irrep[slab_b[0] * B + rep]
    scratch[...] = jnp.zeros_like(scratch)
    for c in range(ROWS):
        label = vir_irrep[red * ROWS + c] ^ b_label
        kept = jnp.where((occ_col ^ label) == occ, integrals[c].astype(F32), 0.0).astype(BF)
        slots = jnp.dot(pick, kept, preferred_element_type=F32)
        for x in range(ACROSS):
            first = (x * PARTS + c // GROUP) * BLOCK + SHARE * (c % GROUP)
            scratch[first : first + SHARE, :O] = slots[x * SHARE : (x + 1) * SHARE]
    for x in range(ACROSS):
        out[x] = scratch[x * PARTS * BLOCK : (x + 1) * PARTS * BLOCK].astype(BF)


def pack_amplitudes(
    place, window, vir_irrep, occ_irrep, slab_a, occ_row, vir_rows, amplitudes, out, starts, chosen, row, packed
):
    red, rep = place()
    step = pl.program_id(0)
    occ = occ_row[...]
    groups = V // GROUP // STACK
    part = NEAR * PARTS

    @pl.when(step == 0)
    def _():
        _, _, pos_col = positions(occ)
        pos_col -= SLOTS * window
        lane = lax.broadcasted_iota(jnp.int32, (O, LANES), 1)
        at = pos_col
        for x in range(1, ACROSS):
            at += jnp.where(pos_col >= x * SHARE, BLOCK - SHARE, 0)
        for u in range(GROUP):
            hit = (lane == at + SHARE * u) & (pos_col >= 0) & (pos_col < SLOTS)
            hit = jnp.concatenate([jnp.where(hit, 1.0, 0.0), jnp.zeros((LANES - O, LANES), F32)], axis=0)
            chosen[u * LANES : (u + 1) * LANES] = hit.astype(BF)
        labels = vir_rows[...]
        for g in range(9):
            below = jnp.sum(jnp.where(labels < g, 1.0, 0.0), axis=1, keepdims=True)
            starts[g : g + 1] = jnp.broadcast_to(below.astype(jnp.int32), (1, LANES))
        for x in range(ACROSS):
            packed[x, pl.ds(ROWS, groups, stride=16), :] = jnp.zeros((groups, LANES), F32)
        row[...] = jnp.zeros_like(row)

    c_index = lax.broadcasted_iota(jnp.int16, (V, O), 0)
    for j in range(STEP):
        row_id = (rep * (FAR * NEAR) + red) * ROWS + step * STEP + j
        label = vir_irrep[slab_a[0] * A + row_id // O] ^ occ_irrep[row_id % O]
        partner = occ ^ label
        low = jnp.zeros((1, O), jnp.int32)
        high = jnp.zeros((1, O), jnp.int32)
        for g in range(8):
            low = jnp.where(partner == g, starts[g : g + 1, :O], low)
            high = jnp.where(partner == g, starts[g + 1 : g + 2, :O], high)
        kept = (c_index >= low.astype(jnp.int16)) & (c_index < high.astype(jnp.int16))
        row[j, :V, :O] = jnp.where(kept, amplitudes[j], jnp.zeros((), BF)).astype(F32)
    for j in range(STEP):
        left = jnp.concatenate(
            [row[j, pl.ds(u, V // GROUP, stride=GROUP), :].astype(BF) for u in range(GROUP)], axis=1
        )
        total = jnp.dot(left, chosen[...], preferred_element_type=F32)
        blocks = [
            jnp.concatenate([total[(STACK * t + f) * part : (STACK * t + f + 1) * part] for t in range(TWICE)], axis=0)
            for f in range(STACK)
        ]
        place_of = lax.broadcasted_iota(jnp.int32, (1, LANES), 1) // BLOCK
        for x in range(ACROSS):
            tile = blocks[0] if x == 0 else pltpu.roll(blocks[0], (LANES - BLOCK * x), 1)
            for f in range(1, STACK):
                moved = blocks[f] if x == f else pltpu.roll(blocks[f], (LANES + BLOCK * (f - x)) % LANES, 1)
                tile = jnp.where(place_of == f, moved, tile)
            packed[x, pl.ds(step * STEP + j, groups, stride=16), :] = tile

    @pl.when(step == ROWS // STEP - 1)
    def _():
        rows = PARTS * 16
        for e in range(NEAR):
            for x in range(ACROSS):
                for t in range(TWICE):
                    first = (t * NEAR + e) * rows
                    out[ACROSS * e + x, t * rows : (t + 1) * rows] = packed[x, first : first + rows].astype(BF)


def slot_owner(place, slot):
    _, rep = place()
    return slot % ACROSS * 2 + (rep + slot // ACROSS) % 2


def multiply(place, window, vir_irrep, slab_a, slab_b, occ_row, amps, *rest):
    ints, (out, kept, picks) = rest[:2], rest[2:]
    red, rep = place()
    occ = occ_row[...]
    rows = TEAM * 16
    left = jnp.concatenate([amps[:, k * 16 : (k + 1) * 16].reshape(rows, LANES) for k in range(DEEP)], axis=1)
    _, _, pos_col = positions(occ)
    occ_lanes = jnp.concatenate([occ, jnp.full((1, LANES - O), 64, jnp.int32)], axis=1)
    pos_col -= SLOTS * window
    pos_col = jnp.where((pos_col >= 0) & (pos_col < SLOTS), pos_col, -4 * LANES)
    pos_lanes = jnp.concatenate([pos_col, jnp.full((LANES - O, 1), -4 * LANES, jnp.int32)], axis=0)
    row = lax.broadcasted_iota(jnp.int32, (rows, LANES), 0)
    i_index = (row // (16 * ACROSS)) * ROWS + row % 16
    row_label = jnp.zeros((rows, LANES), jnp.int32)
    for g in range(1, 8):
        start = jnp.sum(jnp.where(occ < g, 1.0, 0.0), axis=1, keepdims=True).astype(jnp.int32)
        row_label += jnp.where(i_index >= start, 1, 0)
    a_label = jnp.zeros((rows, LANES), jnp.int32)
    for x in range(ACROSS):
        label = vir_irrep[slab_a[0] * A + (x * 2 + rep % 2) * FAR + red // NEAR]
        a_label = jnp.where((row // 16) % ACROSS == x, label, a_label)
    row_label = row_label ^ a_label
    wanted = row_label ^ occ_lanes
    lane = lax.broadcasted_iota(jnp.int32, (LANES, 2 * LANES), 1)
    for slot in range(REP):
        pick = jnp.where(lane == pos_lanes + SLOTS * slot, 1.0, 0.0).astype(BF)
        for piece in range(2):
            first = (2 * slot + piece) * LANES
            picks[first : first + LANES] = pick
    for pair in range(REP // 2):
        held = ints[pair * 2 // ACROSS]
        across = (pair * 2 % ACROSS, pair * 2 % ACROSS + 1)
        right = jnp.concatenate(
            [
                jnp.concatenate([held[far, x, g * BLOCK : (g + 1) * BLOCK] for x in across], axis=1)
                for t in range(TWICE)
                for g in range(PARTS)
                for far in range(t * STACK, (t + 1) * STACK)
            ],
            axis=0,
        )
        both = jnp.dot(left, right, preferred_element_type=F32)
        for half in range(2):
            slot = 2 * pair + half
            b_label = vir_irrep[slab_b[0] * B + slot_owner(place, slot)]
            part = both[:, half * LANES : (half + 1) * LANES]
            part = jnp.where(wanted == b_label, part, 0.0)
            high = part.astype(BF)
            first = 2 * slot * LANES
            kept[:, first : first + LANES] = high
            kept[:, first + LANES : first + 2 * LANES] = (part - high.astype(F32)).astype(BF)
    total = jnp.dot(kept[...], picks[...], preferred_element_type=F32)
    rest = total[:, LANES:]
    moved = pltpu.roll(rest, LANES // 2, 1)
    for e in range(TEAM):
        out[e, :16] = total[e * 16 : (e + 1) * 16, :LANES]
        out[e, 16:] = rest[e * 16 : e * 16 + 8] + moved[e * 16 + 8 : e * 16 + 16]


def finish(
    place, vir_irrep, occ_irrep, slab_a, slab_b, occ_energy, vir_energy, occ_row, energy_row, other, *rest
):
    windows, (out, cycle) = rest[:-2], rest[-2:]
    red, rep = place()
    occ = occ_row[...]
    _, pos_row, _ = positions(occ)
    lane = lax.broadcasted_iota(jnp.int32, (LANES, O), 0)
    values = [jnp.zeros((48, O), F32) for _ in range(REP)]
    for window, parts in enumerate(windows):
        total = parts[0]
        for s in range(1, TEAM):
            total += parts[s]
        main = total[:16]
        rest = jnp.concatenate([total[16:], pltpu.roll(total[16:], LANES // 2, 1)], axis=0)
        mains = jnp.concatenate(thirds(main), axis=0)
        rests = jnp.concatenate(thirds(rest), axis=0)
        at = pos_row - SLOTS * window
        at = jnp.where((at >= 0) & (at < SLOTS), at, -4 * LANES)
        for slot in range(REP):
            if SLOTS * slot < LANES:
                pick = jnp.where(lane == at + SLOTS * slot, 1.0, 0.0).astype(BF)
                values[slot] += jnp.dot(mains, pick, preferred_element_type=F32)
            if SLOTS * (slot + 1) > LANES:
                pick = jnp.where((lane == at + (SLOTS * slot - LANES)) & (lane < LANES // 2), 1.0, 0.0).astype(BF)
                values[slot] += jnp.dot(rests, pick, preferred_element_type=F32)
    for slot in range(REP):
        value = values[slot]
        cycle[pl.ds(slot_owner(place, slot), 16, stride=B), :O] = (value[:16] + value[16:32]) + value[32:]
    b_first = slab_b[0] * B
    b_index = lax.broadcasted_iota(jnp.int32, (B, 1), 0)
    b_label = jnp.zeros((B, 1), jnp.int32)
    b_energy = jnp.zeros((B, 1), F32)
    for b in range(B):
        b_label = jnp.where(b_index == b, vir_irrep[b_first + b], b_label)
        b_energy = jnp.where(b_index == b, vir_energy[b_first + b], b_energy)
    pair_bj = b_label ^ occ
    col_energy = energy_row[...] - b_energy
    for r in range(ROWS):
        row_id = (rep * (FAR * NEAR) + red) * ROWS + r
        a = slab_a[0] * A + row_id // O
        i = row_id % O
        label = vir_irrep[a] ^ occ_irrep[i]
        row_energy = occ_energy[i] - vir_energy[a]
        updated = (cycle[r * B : (r + 1) * B, :O] + other[r]) / (row_energy + col_energy)
        out[r] = jnp.where(pair_bj == label, updated, 0.0)


def own_place():
    return (
        lax.axis_index("far") * NEAR + lax.axis_index("near"),
        lax.axis_index("x") * 2 + lax.axis_index("core"),
    )


SMEM = pl.BlockSpec(memory_space=pltpu.SMEM)
VMEM = pl.BlockSpec(memory_space=pltpu.VMEM)


def params(limit):
    return pltpu.CompilerParams(vmem_limit_bytes=limit * 1024 * 1024)


def call_pack_integrals(place, window, vir_irrep, slab_b, occ_row, integrals):
    return pl.pallas_call(
        functools.partial(pack_integrals, place, window),
        out_shape=(jax.ShapeDtypeStruct((ACROSS, PARTS * BLOCK, LANES), BF), jax.ShapeDtypeStruct((1, 1), jnp.int32)),
        in_specs=[SMEM, SMEM, VMEM, VMEM],
        out_specs=(VMEM, SMEM),
        scratch_shapes=[pltpu.VMEM((ACROSS * PARTS * BLOCK, LANES), F32)],
        compiler_params=params(16),
        cost_estimate=pl.CostEstimate(flops=2 * 10**7, bytes_accessed=600000, transcendentals=0),
        name="pack_integrals",
    )(vir_irrep, slab_b, occ_row, integrals)


def fixed(shape):
    return pl.BlockSpec(shape, lambda step: (0,) * len(shape))


def call_pack_amplitudes(place, window, vir_irrep, occ_irrep, slab_a, occ_row, vir_rows, amplitudes):
    return pl.pallas_call(
        functools.partial(pack_amplitudes, place, window),
        out_shape=jax.ShapeDtypeStruct((TEAM, DEEP * 16, LANES), BF),
        grid=(ROWS // STEP,),
        in_specs=[SMEM, SMEM, SMEM, fixed((1, O)), fixed((1, V)), pl.BlockSpec((STEP, V, O), lambda r: (r, 0, 0))],
        out_specs=fixed((TEAM, DEEP * 16, LANES)),
        scratch_shapes=[
            pltpu.VMEM((16, LANES), jnp.int32),
            pltpu.VMEM((GROUP * LANES, LANES), BF),
            pltpu.VMEM((STEP, V + 8, LANES), F32),
            pltpu.VMEM((ACROSS, V // GROUP // STACK * 16 + 16, LANES), F32),
        ],
        compiler_params=params(16),
        cost_estimate=pl.CostEstimate(flops=10**9, bytes_accessed=4500000, transcendentals=0),
        name="pack_amplitudes",
    )(vir_irrep, occ_irrep, slab_a, occ_row, vir_rows, amplitudes)


def call_multiply(place, window, vir_irrep, slab_a, slab_b, occ_row, amps, ints):
    return pl.pallas_call(
        functools.partial(multiply, place, window),
        out_shape=jax.ShapeDtypeStruct((TEAM, 24, LANES), F32),
        in_specs=[SMEM, SMEM, SMEM, VMEM, VMEM] + [VMEM] * 2,
        out_specs=VMEM,
        scratch_shapes=[
            pltpu.VMEM((TEAM * 16, 2 * REP * LANES), BF),
            pltpu.VMEM((2 * REP * LANES, 2 * LANES), BF),
        ],
        compiler_params=params(24),
        name="multiply",
    )(vir_irrep, slab_a, slab_b, occ_row, amps, *ints)


def call_finish(
    place, vir_irrep, occ_irrep, slab_a, slab_b, occ_energy, vir_energy, occ_row, energy_row, other, windows
):
    return pl.pallas_call(
        functools.partial(finish, place),
        out_shape=jax.ShapeDtypeStruct((ROWS, B, O), F32),
        in_specs=[SMEM] * 6 + [VMEM] * (3 + len(windows)),
        out_specs=VMEM,
        scratch_shapes=[pltpu.VMEM((16 * B + B, LANES), F32)],
        compiler_params=params(16),
        name="finish",
    )(vir_irrep, occ_irrep, slab_a, slab_b, occ_energy, vir_energy, occ_row, energy_row, other, *windows)


def whole_form(amplitudes, integrals, other_terms, occ_energy, vir_energy, occ_irrep, vir_irrep, slab_a, slab_b):
    red, rep = ("far", "near"), ("x", "core")
    red_count = FAR * NEAR
    red_index, rep_index = own_place()
    a_start = slab_a[0] * A
    b_start = slab_b[0] * B
    b_labels = lax.dynamic_slice_in_dim(vir_irrep, b_start, B)
    b_energy = lax.dynamic_slice_in_dim(vir_energy, b_start, B)
    c_labels = lax.dynamic_slice_in_dim(vir_irrep, red_index * ROWS, ROWS)
    pair_ck = pair_labels(c_labels, occ_irrep)
    pair_bj = pair_labels(b_labels, occ_irrep)
    own_pairs = lax.dynamic_slice_in_dim(pair_bj, rep_index, 1, 0)
    local_kept = (pair_ck[:, :, None, None] == own_pairs[None, None]).astype(BF)
    kept = (integrals * local_kept).reshape(1, ROWS * O, O)
    gathered = lax.all_to_all(jnp.broadcast_to(kept, (REP, ROWS * O, O)), rep, 0, 0, tiled=True)
    exchanged = lax.all_to_all(amplitudes, red, split_axis=1, concat_axis=0, tiled=True)
    flat_amps = exchanged.reshape(red_count * ROWS, ROWS * O)
    flat_ints = jnp.swapaxes(gathered, 0, 1).reshape(ROWS * O, B * O)
    parts = jnp.dot(flat_amps, flat_ints, preferred_element_type=F32).reshape(red_count, ROWS, B * O)
    mine = jnp.sum(lax.all_to_all(parts, red, 0, 0, tiled=True), axis=0)
    cycle_term = mine.reshape(ROWS, B, O)
    first_global = (rep_index * red_count + red_index) * ROWS
    row_ids = first_global + jnp.arange(ROWS, dtype=jnp.int32)
    a_index = a_start + row_ids // O
    i_index = row_ids % O
    pair_ai = jnp.bitwise_xor(vir_irrep[a_index], occ_irrep[i_index])
    allowed = pair_ai[:, None, None] == pair_bj[None]
    row_energy = occ_energy[i_index] - vir_energy[a_index]
    col_energy = occ_energy[None, :] - b_energy[:, None]
    denominator = row_energy[:, None, None] + col_energy[None]
    updated = (cycle_term + other_terms) / denominator
    return jnp.where(allowed, updated, jnp.zeros_like(updated))


def window_sums(
    window, count, amplitudes, integrals, occ_irrep, vir_irrep, slab_a, slab_b
):
    occ_row = occ_irrep.reshape(1, O)
    vir_rows = vir_irrep.reshape(1, V)
    ints, most = call_pack_integrals(
        own_place, window, vir_irrep, slab_b, occ_row, integrals.reshape(ROWS, O, O)
    )
    ints = lax.all_to_all(ints, "x", 0, 0, tiled=True)
    amps = call_pack_amplitudes(own_place, window, vir_irrep, occ_irrep, slab_a, occ_row, vir_rows, amplitudes)
    ints = lax.all_gather(ints, "far", axis=0)
    ints, amps = lax.optimization_barrier((ints, amps))
    both = [ints, lax.ppermute(ints, "core", [(0, 1), (1, 0)])]
    amps = lax.all_to_all(amps, ("near", "x"), 0, 0, tiled=True)
    parts = [call_multiply(own_place, col, vir_irrep, slab_a, slab_b, occ_row, amps, both) for col in range(count)]
    return parts, most


def last_step(other_terms, occ_energy, vir_energy, occ_irrep, vir_irrep, slab_a, slab_b, *windows):
    return call_finish(
        own_place, vir_irrep, occ_irrep, slab_a, slab_b, occ_energy, vir_energy,
        occ_irrep.reshape(1, O), occ_energy.reshape(1, O), other_terms, windows,
    )


def two_windows(amplitudes, integrals, other_terms, occ_energy, vir_energy, occ_irrep, vir_irrep, slab_a, slab_b):
    sums = [
        window_sums(window, 2, amplitudes, integrals, occ_irrep, vir_irrep, slab_a, slab_b)[0] for window in range(2)
    ]
    windows = [lax.all_to_all(one + two, ("near", "x"), 0, 0, tiled=True) for one, two in zip(*sums)]
    return last_step(other_terms, occ_energy, vir_energy, occ_irrep, vir_irrep, slab_a, slab_b, *windows)


def on_device(
    amplitudes, integrals, other_terms, occ_energy, vir_energy, occ_irrep, vir_irrep, slab_a, slab_b
):
    args = (amplitudes, integrals, other_terms, occ_energy, vir_energy, occ_irrep, vir_irrep, slab_a, slab_b)
    (parts,), most = window_sums(0, 1, amplitudes, integrals, occ_irrep, vir_irrep, slab_a, slab_b)
    parts, most = lax.optimization_barrier((parts, most[0, 0]))
    parts = lax.all_to_all(parts, ("near", "x"), 0, 0, tiled=True)

    def crowded(*rest):
        return lax.cond(most >= 2 * SLOTS, whole_form, two_windows, *rest[:-1])

    return lax.cond(most >= SLOTS, crowded, lambda *rest: last_step(*rest[2:]), *args, parts)


def solution(mesh):
    split = Mesh(mesh.devices.reshape(FAR, NEAR, ACROSS, 2), ("far", "near", "x", "core"))
    rows = P(("x", "core", "far", "near"), None, None)
    placed = (
        rows,
        P(("far", "near"), None, ("x", "core"), None),
        rows,
        P(),
        P(),
        P(),
        P(),
        P(),
        P(),
    )
    return jax.shard_map(
        on_device,
        mesh=split,
        in_specs=placed,
        out_specs=rows,
        check_vma=False,
    )
```

profile of v0, /device:TPU:6, one launch (start us, length us, event | category | flops | bytes accessed | tf_op | source)
XLA Modules:
  0.0 91.3 jit_solution(573914933836695769)
XLA Ops:
  0.7 2.1 %pack_integrals.5 = (bf16[4,96,128]{2,1,0:T(8,128)(2,1)}, s32[1,1]{1,0:T(1,128)}) custom-call(s32[960]{0:T(1024)} %vir_irrep.5, s32[1]{0:T(128)S(6)} %copy.30.slab_b, s32[1,120]{1,0:T(1,128)} %bitcast.42, bf16[15,120,120]{2,1,0:T(8,128)(2,1)} %bitcast.60), custom_call_target="tpu_custom_call" | custom-call | flops 20000000 | bytes 600000 | tf_op jit(solution)/shard_map/pack_integrals/pallas_call | solution.py:279
  2.7 0.0 copy-start.8
  2.7 0.0 copy-start.10
  2.7 9.1 %all-to-all-start.9 = ((bf16[4,96,128]{2,1,0:T(8,128)(2,1)}), bf16[4,96,128]{2,1,0:T(8,128)(2,1)S(1)}, u32[]{:S(2)}, u32[]{:S(2)}) async-start(bf16[4,96,128]{2,1,0:T(8,128)(2,1)} %get-tuple-element.131), calls=%async_computation.9 | async-start | bytes 196608 | tf_op jit(solution)/shard_map/all_to_all | solution.py:385
  12.5 6.0 %pack_amplitudes.5 = bf16[32,96,128]{2,1,0:T(8,128)(2,1)} custom-call(s32[960]{0:T(1024)} %vir_irrep.5, s32[120]{0:T(128)} %occ_irrep.1, s32[1]{0:T(128)S(6)} %copy.29.slab_a, s32[1,120]{1,0:T(1,128)} %bitcast.43, s32[1,960]{1,0:T(1,128)} %bitcast.57, bf16[15,960,120]{2,1,0:T(8,128)(2,1)} %amplitudes.1), custom_call_target="tpu_custom_call" | custom-call | flops 1000000000 | bytes 4500000 | tf_op jit(solution)/shard_map/pack_amplitudes/pallas_call | solution.py:296
  18.5 0.0 copy-start.9
  18.5 0.0 copy-start.11
  18.5 0.0 copy-start.12
  18.5 0.0 copy-start.13
  18.5 0.0 all-to-all-done.9
  18.5 34.3 %all-gather.2 = bf16[32,96,128]{2,1,0:T(8,128)(2,1)S(1)} all-gather(bf16[4,96,128]{2,1,0:T(8,128)(2,1)S(1)} %all-to-all-done.9), channel_id=4, replica_groups=mesh['far'=8,'near'=8,'x'=4,'core'=2] {'far'}, dimensions={0}, use_global_device_ids=true | all-gather | bytes 884736 | tf_op jit(solution)/shard_map/all_gather | solution.py:387
  52.9 8.5 %all-to-all-start.10 = ((bf16[32,96,128]{2,1,0:T(8,128)(2,1)}), bf16[32,96,128]{2,1,0:T(8,128)(2,1)S(1)}, u32[]{:S(2)}, u32[]{:S(2)}) async-start(bf16[32,96,128]{2,1,0:T(8,128)(2,1)} %pack_amplitudes.5), calls=%async_computation.10 | async-start | bytes 1572864 | tf_op jit(solution)/shard_map/all_to_all | solution.py:390
  61.4 1.9 %collective-permute-start.2 = (bf16[8,4,96,128]{3,2,1,0:T(8,128)(2,1)S(1)}, bf16[8,4,96,128]{3,2,1,0:T(8,128)(2,1)S(1)}, u32[]{:S(2)}, u32[]{:S(2)}) collective-permute-start(bf16[8,4,96,128]{3,2,1,0:T(8,128)(2,1)S(1)} %bitcast.40), channel_id=1, source_target_pairs={{0,1},{1,0},{2,3},{3,2},{4,5},{5,4},{6,7},{7,6},{8,9},{9,8},{10,11... | collective-permute-start | bytes 2359304 | tf_op jit(solution)/shard_map/ppermute | solution.py:389
  63.3 2.3 %collective-permute-done.2.rest_1_ = bf16[8,4,96,128]{3,2,1,0:T(8,128)(2,1)S(1)} collective-permute-done((bf16[8,4,96,128]{3,2,1,0:T(8,128)(2,1)S(1)}, bf16[8,4,96,128]{3,2,1,0:T(8,128)(2,1)S(1)}, u32[]{:S(2)}, u32[]{:S(2)}) %collective-permute-start.2) | collective-permute-done | bytes 786464 | tf_op jit(solution)/shard_map/ppermute | solution.py:389
  65.6 5.5 %all-to-all-done.10.amps = bf16[32,96,128]{2,1,0:T(8,128)(2,1)S(1)} async-done(((bf16[32,96,128]{2,1,0:T(8,128)(2,1)}), bf16[32,96,128]{2,1,0:T(8,128)(2,1)S(1)}, u32[]{:S(2)}, u32[]{:S(2)}) %all-to-all-start.10) | async-done | bytes 786464 | tf_op jit(solution)/shard_map/all_to_all | solution.py:390
  71.0 0.0 copy-done.8
  71.0 0.0 copy-done.10
  71.0 3.4 %multiply.9 = f32[32,24,128]{2,1,0:T(8,128)} custom-call(s32[960]{0:T(1024)S(1)} %copy-done.10, s32[1]{0:T(128)S(6)} %copy.29.slab_a, s32[1]{0:T(128)S(6)} %copy.30.slab_b, s32[1,120]{1,0:T(1,128)S(1)} %bitcast.44, bf16[32,96,128]{2,1,0:T(8,128)(2,1)S(1)} %all-to-all-done.10.amps, bf16[8,4,96,128]{3,2,1,0:T(8,128)(2,1)S(1)} %bitcast.41, ...), custom_call_target="tpu_custom_call" | custom-call | tf_op jit(solution)/shard_map/multiply/pallas_call | solution.py:315
  74.5 5.8 %all-to-all-start.11 = ((f32[32,24,128]{2,1,0:T(8,128)}), f32[32,24,128]{2,1,0:T(8,128)S(1)}, u32[]{:S(2)}, u32[]{:S(2)}) async-start(f32[32,24,128]{2,1,0:T(8,128)} %multiply.9), calls=%async_computation.11 | async-start | bytes 786432 | tf_op jit(solution)/shard_map/all_to_all | solution.py:416
  80.9 7.3 %all-to-all-done.11 = f32[32,24,128]{2,1,0:T(8,128)S(1)} async-done(((f32[32,24,128]{2,1,0:T(8,128)}), f32[32,24,128]{2,1,0:T(8,128)S(1)}, u32[]{:S(2)}, u32[]{:S(2)}) %all-to-all-start.11) | async-done | bytes 393248 | tf_op jit(solution)/shard_map/all_to_all | solution.py:416
  88.3 0.0 copy-done.9
  88.3 0.0 copy-done.11
  88.3 0.0 copy-done.12
  88.3 0.0 copy-done.13
  88.3 3.0 %conditional.2 = (f32[15,8,120]{2,1,0:T(8,128)}) conditional(s32[]{:T(128)} %convert_element_type.7, (s32[120]{0:T(128)S(1)}, f32[120]{0:T(128)S(1)}, s32[960]{0:T(1024)S(1)}, s32[1]{0:T(128)}, s32[1]{0:T(128)}, /*index=5*/f32[960]{0:T(1024)S(1)}, f32[15,8,120]{2,1,0:T(8,128)S(1)}, f32[32,24,128]{2,1,0:T(8,128)S(1)}) %tuple.48, (s32[]{:T(128)}, ...), branch_computations={%region_0.0_spmd, %region_1.5_spmd} | conditional | flops 3319177216 | bytes 88702576 | solution.py:421
  88.3 3.0 %finish.2 = f32[15,8,120]{2,1,0:T(8,128)} custom-call(s32[960]{0:T(1024)S(1)} %get-tuple-element.82.vir_irrep, s32[120]{0:T(128)S(1)} %get-tuple-element.84.occ_irrep, s32[1]{0:T(128)} %get-tuple-element.85.slab_a, s32[1]{0:T(128)} %get-tuple-element.86.slab_b, f32[120]{0:T(128)S(1)} %get-tuple-element.87.occ_energy, f32[960]{0:T(1024)S(1)} %get-tuple-element.88.vir_energy, ...), custom_call_target="tpu_custom_call" | custom-call | tf_op jit(solution)/shard_map/cond/branch_0_fun/finish/pallas_call | solution.py:332
Async XLA Ops:
  2.7 68.3 %copy-start.8 = (s32[120]{0:T(128)S(1)}, s32[120]{0:T(128)}, u32[]{:S(2)}) copy-start(s32[120]{0:T(128)} %occ_irrep.1) | copy-start | bytes 1444
  2.7 68.3 %copy-start.10 = (s32[960]{0:T(1024)S(1)}, s32[960]{0:T(1024)}, u32[]{:S(2)}) copy-start(s32[960]{0:T(1024)} %vir_irrep.5) | copy-start | bytes 11524
  2.7 15.8 %all-to-all-start.9 = ((bf16[4,96,128]{2,1,0:T(8,128)(2,1)}), bf16[4,96,128]{2,1,0:T(8,128)(2,1)S(1)}, u32[]{:S(2)}, u32[]{:S(2)}) async-start(bf16[4,96,128]{2,1,0:T(8,128)(2,1)} %get-tuple-element.131), calls=%async_computation.9 | async-start | bytes 196608 | tf_op jit(solution)/shard_map/all_to_all | solution.py:385
  18.5 69.8 %copy-start.9 = (f32[120]{0:T(128)S(1)}, f32[120]{0:T(128)}, u32[]{:S(2)}) copy-start(f32[120]{0:T(128)} %param.16) | copy-start | bytes 1444
  18.5 69.8 %copy-start.11 = (f32[960]{0:T(1024)S(1)}, f32[960]{0:T(1024)}, u32[]{:S(2)}) copy-start(f32[960]{0:T(1024)} %param.17) | copy-start | bytes 11524
  18.5 69.8 %copy-start.12 = (bf16[15,120,1,120]{3,1,2,0:T(8,128)(2,1)S(1)}, bf16[15,120,1,120]{3,1,2,0:T(8,128)(2,1)}, u32[]{:S(2)}) copy-start(bf16[15,120,1,120]{3,1,2,0:T(8,128)(2,1)} %param.14) | copy-start | bytes 1296004
  18.5 69.8 %copy-start.13 = (f32[15,8,120]{2,1,0:T(8,128)S(1)}, f32[15,8,120]{2,1,0:T(8,128)}, u32[]{:S(2)}) copy-start(f32[15,8,120]{2,1,0:T(8,128)} %param.15) | copy-start | bytes 172804
  52.9 18.1 %all-to-all-start.10 = ((bf16[32,96,128]{2,1,0:T(8,128)(2,1)}), bf16[32,96,128]{2,1,0:T(8,128)(2,1)S(1)}, u32[]{:S(2)}, u32[]{:S(2)}) async-start(bf16[32,96,128]{2,1,0:T(8,128)(2,1)} %pack_amplitudes.5), calls=%async_computation.10 | async-start | bytes 1572864 | tf_op jit(solution)/shard_map/all_to_all | solution.py:390
  61.4 4.2 %collective-permute-start.2 = (bf16[8,4,96,128]{3,2,1,0:T(8,128)(2,1)S(1)}, bf16[8,4,96,128]{3,2,1,0:T(8,128)(2,1)S(1)}, u32[]{:S(2)}, u32[]{:S(2)}) collective-permute-start(bf16[8,4,96,128]{3,2,1,0:T(8,128)(2,1)S(1)} %bitcast.40), channel_id=1, source_target_pairs={{0,1},{1,0},{2,3},{3,2},{4,5},{5,4},{6,7},{7,6},{8,9},{9,8},{10,11... | collective-permute-start | bytes 2359304 | tf_op jit(solution)/shard_map/ppermute | solution.py:389
  74.5 13.8 %all-to-all-start.11 = ((f32[32,24,128]{2,1,0:T(8,128)}), f32[32,24,128]{2,1,0:T(8,128)S(1)}, u32[]{:S(2)}, u32[]{:S(2)}) async-start(f32[32,24,128]{2,1,0:T(8,128)} %multiply.9), calls=%async_computation.11 | async-start | bytes 786432 | tf_op jit(solution)/shard_map/all_to_all | solution.py:416
where the time goes:
time: 92.3 us; the launch traced here: 91.3 us
  blocking collectives  34.3 us (37%)
  starting transfers between devices  25.4 us (28%)
  waiting for transfers between devices  15 us (16%)
  Pallas kernels  14.5 us (16%)
  between operations  2.02 us (2%)
    all_gather x1, blocking collectives, window_sums(): ints = lax.all_gather(ints, 'far', axis=0)  34.3 us
    all_to_all x1, starting transfers between devices, window_sums(): ints = lax.all_to_all(ints, 'x', 0, 0, tiled=True)  9.14 us
    all_to_all x1, starting transfers between devices, window_sums(): amps = lax.all_to_all(amps, ('near', 'x'), 0, 0, tiled=True)  8.51 us
    all_to_all x1, waiting for transfers between devices, on_device(): parts = lax.all_to_all(parts, ('near', 'x'), 0, 0, tiled=True)  7.33 us
    pallas_call x1, Pallas kernels, call_pack_amplitudes(): pl.pallas_call(functools.partial(pack_amplitudes, place, window), out_sha...  5.97 us
    all_to_all x1, starting transfers between devices, on_device(): parts = lax.all_to_all(parts, ('near', 'x'), 0, 0, tiled=True)  5.83 us
    all_to_all x1, waiting for transfers between devices, window_sums(): amps = lax.all_to_all(amps, ('near', 'x'), 0, 0, tiled=True)  5.45 us
    pallas_call x1, Pallas kernels, call_multiply(): pl.pallas_call(functools.partial(multiply, place, window), out_shape=jax....  3.44 us
  transfers between devices with their start and end apart: 4, of which 3 were waited for; matrix products, arithmetic and copies ran while one was open for 0% of the time, Pallas kernels for 7%

commit v1 on v0

--- a/solution.py
+++ b/solution.py
@@ -81,7 +81,7 @@
 
 
 def pack_amplitudes(
-    place, window, vir_irrep, occ_irrep, slab_a, occ_row, vir_rows, amplitudes, out, starts, chosen, row, packed
+    place, window, vir_irrep, occ_irrep, slab_a, occ_row, vir_rows, first_half, second_half, out, starts, chosen, row, packed
 ):
     red, rep = place()
     step = pl.program_id(0)
@@ -120,7 +120,9 @@
             low = jnp.where(partner == g, starts[g : g + 1, :O], low)
             high = jnp.where(partner == g, starts[g + 1 : g + 2, :O], high)
         kept = (c_index >= low.astype(jnp.int16)) & (c_index < high.astype(jnp.int16))
-        row[j, :V, :O] = jnp.where(kept, amplitudes[j], jnp.zeros((), BF)).astype(F32)
+        for half, part_of in enumerate((first_half, second_half)):
+            at = slice(half * V // 2, (half + 1) * V // 2)
+            row[j, at, :O] = jnp.where(kept[at], part_of[j], jnp.zeros((), BF)).astype(F32)
     for j in range(STEP):
         left = jnp.concatenate(
             [row[j, pl.ds(u, V // GROUP, stride=GROUP), :].astype(BF) for u in range(GROUP)], axis=1
@@ -297,7 +299,7 @@
         functools.partial(pack_amplitudes, place, window),
         out_shape=jax.ShapeDtypeStruct((TEAM, DEEP * 16, LANES), BF),
         grid=(ROWS // STEP,),
-        in_specs=[SMEM, SMEM, SMEM, fixed((1, O)), fixed((1, V)), pl.BlockSpec((STEP, V, O), lambda r: (r, 0, 0))],
+        in_specs=[SMEM, SMEM, SMEM, fixed((1, O)), fixed((1, V)), pl.BlockSpec((STEP, V // 2, O), lambda r: (r, 0, 0)), pl.BlockSpec((STEP, V // 2, O), lambda r: (r, 1, 0))],
         out_specs=fixed((TEAM, DEEP * 16, LANES)),
         scratch_shapes=[
             pltpu.VMEM((16, LANES), jnp.int32),
@@ -308,7 +310,7 @@
         compiler_params=params(16),
         cost_estimate=pl.CostEstimate(flops=10**9, bytes_accessed=4500000, transcendentals=0),
         name="pack_amplitudes",
-    )(vir_irrep, occ_irrep, slab_a, occ_row, vir_rows, amplitudes)
+    )(vir_irrep, occ_irrep, slab_a, occ_row, vir_rows, amplitudes, amplitudes)
 
 
 def call_multiply(place, window, vir_irrep, slab_a, slab_b, occ_row, amps, ints):

time: 92.3 us -> 92.4 us (level)
  no operation moved by 1% of the time
where the time goes in v1:
time: 92.4 us; the launch traced here: 91.4 us
  blocking collectives  34.4 us (37%)
  starting transfers between devices  25.4 us (27%)
  waiting for transfers between devices  15 us (16%)
  Pallas kernels  14.6 us (16%)
  between operations  2.03 us (2%)
    all_gather x1, blocking collectives, window_sums(): ints = lax.all_gather(ints, 'far', axis=0)  34.4 us
    all_to_all x1, starting transfers between devices, window_sums(): ints = lax.all_to_all(ints, 'x', 0, 0, tiled=True)  9.14 us
    all_to_all x1, starting transfers between devices, window_sums(): amps = lax.all_to_all(amps, ('near', 'x'), 0, 0, tiled=True)  8.5 us
    all_to_all x1, waiting for transfers between devices, on_device(): parts = lax.all_to_all(parts, ('near', 'x'), 0, 0, tiled=True)  7.33 us
    pallas_call x1, Pallas kernels, call_pack_amplitudes(): pl.pallas_call(functools.partial(pack_amplitudes, place, window), out_sha...  6.09 us
    all_to_all x1, starting transfers between devices, on_device(): parts = lax.all_to_all(parts, ('near', 'x'), 0, 0, tiled=True)  5.83 us
    all_to_all x1, waiting for transfers between devices, window_sums(): amps = lax.all_to_all(amps, ('near', 'x'), 0, 0, tiled=True)  5.45 us
    pallas_call x1, Pallas kernels, call_multiply(): pl.pallas_call(functools.partial(multiply, place, window), out_shape=jax....  3.44 us
  transfers between devices with their start and end apart: 4, of which 3 were waited for; matrix products, arithmetic and copies ran while one was open for 0% of the time, Pallas kernels for 7%

profile of v1, /device:TPU:6, one launch (start us, length us, event | category | flops | bytes accessed | tf_op | source)
XLA Modules:
  0.0 91.4 jit_solution(5902028992946512270)
XLA Ops:
  0.7 2.1 %pack_integrals.5 = (bf16[4,96,128]{2,1,0:T(8,128)(2,1)}, s32[1,1]{1,0:T(1,128)}) custom-call(s32[960]{0:T(1024)} %vir_irrep.5, s32[1]{0:T(128)S(6)} %copy.30.slab_b, s32[1,120]{1,0:T(1,128)} %bitcast.42, bf16[15,120,120]{2,1,0:T(8,128)(2,1)} %bitcast.60), custom_call_target="tpu_custom_call" | custom-call | flops 20000000 | bytes 600000 | tf_op jit(solution)/shard_map/pack_integrals/pallas_call | solution.py:281
  2.7 9.1 %all-to-all-start.9 = ((bf16[4,96,128]{2,1,0:T(8,128)(2,1)}), bf16[4,96,128]{2,1,0:T(8,128)(2,1)S(1)}, u32[]{:S(2)}, u32[]{:S(2)}) async-start(bf16[4,96,128]{2,1,0:T(8,128)(2,1)} %get-tuple-element.131), calls=%async_computation.9 | async-start | bytes 196608 | tf_op jit(solution)/shard_map/all_to_all | solution.py:387
  12.5 0.0 copy-start.8
  12.5 0.0 copy-start.10
  12.5 6.1 %pack_amplitudes.5 = bf16[32,96,128]{2,1,0:T(8,128)(2,1)} custom-call(s32[960]{0:T(1024)} %vir_irrep.5, s32[120]{0:T(128)} %occ_irrep.1, s32[1]{0:T(128)S(6)} %copy.29.slab_a, s32[1,120]{1,0:T(1,128)} %bitcast.43, s32[1,960]{1,0:T(1,128)} %bitcast.57, bf16[15,960,120]{2,1,0:T(8,128)(2,1)} %second_half.1, bf16[15,960,120]{2,1,0:T(8,128)(2,1)} %second_half.1), custom_call_target="tpu_custom_call" | custom-call | flops 1000000000 | bytes 4500000 | tf_op jit(solution)/shard_map/pack_amplitudes/pallas_call | solution.py:298
  18.6 0.0 copy-start.9
  18.6 0.0 copy-start.11
  18.6 0.0 copy-start.12
  18.6 0.0 copy-start.13
  18.6 0.0 all-to-all-done.9
  18.7 34.4 %all-gather.2 = bf16[32,96,128]{2,1,0:T(8,128)(2,1)S(1)} all-gather(bf16[4,96,128]{2,1,0:T(8,128)(2,1)S(1)} %all-to-all-done.9), channel_id=4, replica_groups=mesh['far'=8,'near'=8,'x'=4,'core'=2] {'far'}, dimensions={0}, use_global_device_ids=true | all-gather | bytes 884736 | tf_op jit(solution)/shard_map/all_gather | solution.py:389
  53.0 8.5 %all-to-all-start.10 = ((bf16[32,96,128]{2,1,0:T(8,128)(2,1)}), bf16[32,96,128]{2,1,0:T(8,128)(2,1)S(1)}, u32[]{:S(2)}, u32[]{:S(2)}) async-start(bf16[32,96,128]{2,1,0:T(8,128)(2,1)} %pack_amplitudes.5), calls=%async_computation.10 | async-start | bytes 1572864 | tf_op jit(solution)/shard_map/all_to_all | solution.py:392
  61.5 1.9 %collective-permute-start.2 = (bf16[8,4,96,128]{3,2,1,0:T(8,128)(2,1)S(1)}, bf16[8,4,96,128]{3,2,1,0:T(8,128)(2,1)S(1)}, u32[]{:S(2)}, u32[]{:S(2)}) collective-permute-start(bf16[8,4,96,128]{3,2,1,0:T(8,128)(2,1)S(1)} %bitcast.40), channel_id=1, source_target_pairs={{0,1},{1,0},{2,3},{3,2},{4,5},{5,4},{6,7},{7,6},{8,9},{9,8},{10,11... | collective-permute-start | bytes 2359304 | tf_op jit(solution)/shard_map/ppermute | solution.py:391
  63.4 2.3 %collective-permute-done.2.rest_1_ = bf16[8,4,96,128]{3,2,1,0:T(8,128)(2,1)S(1)} collective-permute-done((bf16[8,4,96,128]{3,2,1,0:T(8,128)(2,1)S(1)}, bf16[8,4,96,128]{3,2,1,0:T(8,128)(2,1)S(1)}, u32[]{:S(2)}, u32[]{:S(2)}) %collective-permute-start.2) | collective-permute-done | bytes 786464 | tf_op jit(solution)/shard_map/ppermute | solution.py:391
  65.7 5.5 %all-to-all-done.10.amps = bf16[32,96,128]{2,1,0:T(8,128)(2,1)S(1)} async-done(((bf16[32,96,128]{2,1,0:T(8,128)(2,1)}), bf16[32,96,128]{2,1,0:T(8,128)(2,1)S(1)}, u32[]{:S(2)}, u32[]{:S(2)}) %all-to-all-start.10) | async-done | bytes 786464 | tf_op jit(solution)/shard_map/all_to_all | solution.py:392
  71.2 0.0 copy-done.8
  71.2 0.0 copy-done.10
  71.2 3.4 %multiply.9 = f32[32,24,128]{2,1,0:T(8,128)} custom-call(s32[960]{0:T(1024)S(1)} %copy-done.10, s32[1]{0:T(128)S(6)} %copy.29.slab_a, s32[1]{0:T(128)S(6)} %copy.30.slab_b, s32[1,120]{1,0:T(1,128)S(1)} %bitcast.44, bf16[32,96,128]{2,1,0:T(8,128)(2,1)S(1)} %all-to-all-done.10.amps, bf16[8,4,96,128]{3,2,1,0:T(8,128)(2,1)S(1)} %bitcast.41, ...), custom_call_target="tpu_custom_call" | custom-call | tf_op jit(solution)/shard_map/multiply/pallas_call | solution.py:317
  74.6 5.8 %all-to-all-start.11 = ((f32[32,24,128]{2,1,0:T(8,128)}), f32[32,24,128]{2,1,0:T(8,128)S(1)}, u32[]{:S(2)}, u32[]{:S(2)}) async-start(f32[32,24,128]{2,1,0:T(8,128)} %multiply.9), calls=%async_computation.11 | async-start | bytes 786432 | tf_op jit(solution)/shard_map/all_to_all | solution.py:418
  81.1 7.3 %all-to-all-done.11 = f32[32,24,128]{2,1,0:T(8,128)S(1)} async-done(((f32[32,24,128]{2,1,0:T(8,128)}), f32[32,24,128]{2,1,0:T(8,128)S(1)}, u32[]{:S(2)}, u32[]{:S(2)}) %all-to-all-start.11) | async-done | bytes 393248 | tf_op jit(solution)/shard_map/all_to_all | solution.py:418
  88.4 0.0 copy-done.9
  88.4 0.0 copy-done.11
  88.4 0.0 copy-done.12
  88.4 0.0 copy-done.13
  88.4 3.0 %conditional.2 = (f32[15,8,120]{2,1,0:T(8,128)}) conditional(s32[]{:T(128)} %convert_element_type.7, (s32[120]{0:T(128)S(1)}, f32[120]{0:T(128)S(1)}, s32[960]{0:T(1024)S(1)}, s32[1]{0:T(128)}, s32[1]{0:T(128)}, /*index=5*/f32[960]{0:T(1024)S(1)}, f32[15,8,120]{2,1,0:T(8,128)S(1)}, f32[32,24,128]{2,1,0:T(8,128)S(1)}) %tuple.48, (s32[]{:T(128)}, ...), branch_computations={%region_0.0_spmd, %region_1.5_spmd} | conditional | flops 3319177216 | bytes 88702576 | solution.py:423
  88.4 3.0 %finish.2 = f32[15,8,120]{2,1,0:T(8,128)} custom-call(s32[960]{0:T(1024)S(1)} %get-tuple-element.82.vir_irrep, s32[120]{0:T(128)S(1)} %get-tuple-element.84.occ_irrep, s32[1]{0:T(128)} %get-tuple-element.85.slab_a, s32[1]{0:T(128)} %get-tuple-element.86.slab_b, f32[120]{0:T(128)S(1)} %get-tuple-element.87.occ_energy, f32[960]{0:T(1024)S(1)} %get-tuple-element.88.vir_energy, ...), custom_call_target="tpu_custom_call" | custom-call | tf_op jit(solution)/shard_map/cond/branch_0_fun/finish/pallas_call | solution.py:334
Async XLA Ops:
  2.7 15.9 %all-to-all-start.9 = ((bf16[4,96,128]{2,1,0:T(8,128)(2,1)}), bf16[4,96,128]{2,1,0:T(8,128)(2,1)S(1)}, u32[]{:S(2)}, u32[]{:S(2)}) async-start(bf16[4,96,128]{2,1,0:T(8,128)(2,1)} %get-tuple-element.131), calls=%async_computation.9 | async-start | bytes 196608 | tf_op jit(solution)/shard_map/all_to_all | solution.py:387
  12.5 58.7 %copy-start.8 = (s32[120]{0:T(128)S(1)}, s32[120]{0:T(128)}, u32[]{:S(2)}) copy-start(s32[120]{0:T(128)} %occ_irrep.1) | copy-start | bytes 1444
  12.5 58.6 %copy-start.10 = (s32[960]{0:T(1024)S(1)}, s32[960]{0:T(1024)}, u32[]{:S(2)}) copy-start(s32[960]{0:T(1024)} %vir_irrep.5) | copy-start | bytes 11524
  18.6 69.8 %copy-start.9 = (f32[120]{0:T(128)S(1)}, f32[120]{0:T(128)}, u32[]{:S(2)}) copy-start(f32[120]{0:T(128)} %param.16) | copy-start | bytes 1444
  18.6 69.8 %copy-start.11 = (f32[960]{0:T(1024)S(1)}, f32[960]{0:T(1024)}, u32[]{:S(2)}) copy-start(f32[960]{0:T(1024)} %param.17) | copy-start | bytes 11524
  18.6 69.8 %copy-start.12 = (bf16[15,120,1,120]{3,1,2,0:T(8,128)(2,1)S(1)}, bf16[15,120,1,120]{3,1,2,0:T(8,128)(2,1)}, u32[]{:S(2)}) copy-start(bf16[15,120,1,120]{3,1,2,0:T(8,128)(2,1)} %param.14) | copy-start | bytes 1296004
  18.6 69.8 %copy-start.13 = (f32[15,8,120]{2,1,0:T(8,128)S(1)}, f32[15,8,120]{2,1,0:T(8,128)}, u32[]{:S(2)}) copy-start(f32[15,8,120]{2,1,0:T(8,128)} %param.15) | copy-start | bytes 172804
  53.0 18.1 %all-to-all-start.10 = ((bf16[32,96,128]{2,1,0:T(8,128)(2,1)}), bf16[32,96,128]{2,1,0:T(8,128)(2,1)S(1)}, u32[]{:S(2)}, u32[]{:S(2)}) async-start(bf16[32,96,128]{2,1,0:T(8,128)(2,1)} %pack_amplitudes.5), calls=%async_computation.10 | async-start | bytes 1572864 | tf_op jit(solution)/shard_map/all_to_all | solution.py:392
  61.5 4.2 %collective-permute-start.2 = (bf16[8,4,96,128]{3,2,1,0:T(8,128)(2,1)S(1)}, bf16[8,4,96,128]{3,2,1,0:T(8,128)(2,1)S(1)}, u32[]{:S(2)}, u32[]{:S(2)}) collective-permute-start(bf16[8,4,96,128]{3,2,1,0:T(8,128)(2,1)S(1)} %bitcast.40), channel_id=1, source_target_pairs={{0,1},{1,0},{2,3},{3,2},{4,5},{5,4},{6,7},{7,6},{8,9},{9,8},{10,11... | collective-permute-start | bytes 2359304 | tf_op jit(solution)/shard_map/ppermute | solution.py:391
  74.6 13.8 %all-to-all-start.11 = ((f32[32,24,128]{2,1,0:T(8,128)}), f32[32,24,128]{2,1,0:T(8,128)S(1)}, u32[]{:S(2)}, u32[]{:S(2)}) async-start(f32[32,24,128]{2,1,0:T(8,128)} %multiply.9), calls=%async_computation.11 | async-start | bytes 786432 | tf_op jit(solution)/shard_map/all_to_all | solution.py:418
